TPU v7x, 32 devices: a whole 2x2x4 slice. The times are simulated.
32 devices in a mesh: dp: 32 (over z, y, x, core).
Axes of the slice: x: 2, y: 2, z: 4, core: 2. Of those that a mesh axis runs over, the one named last changes fastest.
Arguments:
- images: bfloat16 [2, 32, 784, 512], P(None, 'dp'), may hold values from -6 to 6
- cotangent: bfloat16 [2, 32, 784, 512], P(None, 'dp'), may hold values from -0.23925781 to 0.23925781
- w_reduce: float32 [32, 65536], P('dp'), may hold values from -0.5 to 0.5
- w_spatial: float32 [32, 147456], P('dp'), may hold values from -0.3125 to 0.3125
- w_expand: float32 [32, 65536], P('dp'), may hold values from -1 to 1
- norm_gain: float32 [32, 768], P('dp'), may hold values from 0.5 to 1.5
- norm_bias: float32 [32, 768], P('dp'), may hold values from -1.2 to 1.2
- round_index: int32 [1], replicated, may hold values from 0 to 63
Outputs:
- avg_reduce: float32 [65536], P('dp')
- avg_spatial: float32 [147456], P('dp')
- avg_expand: float32 [65536], P('dp')
- avg_norm: float32 [1536], P('dp')
- moment_reduce: bfloat16 [32, 65536], P('dp')
- moment_spatial: bfloat16 [32, 147456], P('dp')
- moment_expand: bfloat16 [32, 65536], P('dp')
- moment_norm: bfloat16 [32, 1536], P('dp')
All inputs are finite; a program needn't handle non-finite values.
Results may differ from a plain program's by a relative error of at most 0.017.
Values sent between devices are 32-bit elements; how exact they have to be, the bound alone decides.
No kernel may reach another device: no remote copies, remote signals or barrier semaphores. Data moves between devices by JAX's collectives and lax.ppermute only.
A program may use at most 64 MiB of HBM per device.

v0:
```python
import functools

import jax
import jax.numpy as jnp
from jax import lax
from jax.experimental import pallas as pl
from jax.experimental.pallas import tpu as pltpu
from jax.sharding import PartitionSpec as P

HEIGHT = 28
WIDTH = 28
KSIZE = 3

LEARN_RATE = 0.01
MOMENTUM = 0.9
EPSILON = 1e-05

LANES = 128
PITCH = 32
VMEM_BYTES = 60 * 1024 * 1024
SMALL_VMEM = 8 * 1024 * 1024


def round_up(value, unit):
    return (value + unit - 1) // unit * unit


def partner_2(value, axis, distance):
    mask = 2**distance
    pairs = [(source, source ^ mask) for source in range(lax.axis_size(axis))]
    return lax.ppermute(value, axis, pairs)


def matmul(left, right):
    return jnp.dot(left, right, preferred_element_type=jnp.float32)


def contract_cols(left, right):
    return lax.dot_general(left, right, (((1,), (1,)), ((), ())), preferred_element_type=jnp.float32)


def activate_half(half):
    return half * (1.0 + jnp.tanh(half))


def twice_slope(half):
    bend = jnp.tanh(half)
    return (1.0 + bend) * (1.0 + half * (1.0 - bend))


def column_sum(values):
    return jnp.sum(values, axis=0, keepdims=True)


MAPS = 4
FLAT = MAPS * WIDTH
PITCHED = MAPS * PITCH
CHUNKS = HEIGHT // MAPS
SPAN = KSIZE * LANES
TOP = PITCH
TOP_BACK = 2 * PITCH
ROWS = round_up(HEIGHT * PITCH + 2 * PITCH, LANES)
ROWS_BACK = ROWS + 2 * PITCH


def flat_rows(at):
    return pl.ds(pl.multiple_of(at * FLAT, FLAT), FLAT)


def zero_row(width):
    return jnp.zeros((1, width), jnp.float32)


def sweep(body, init=0, unroll=True):
    return lax.fori_loop(0, CHUNKS, body, init, unroll=unroll)


def fold_rows(values):
    rows, width = values.shape
    return jnp.sum(values.reshape(rows // 8, 8, width), axis=0)


def zero_rows(width):
    return jnp.zeros((8, width), jnp.float32)


def statistics(values_ref, total):
    count, width = values_ref.shape
    mean = column_sum(total) / count

    def add(at, held):
        center = values_ref[flat_rows(at), :] - mean
        return held + fold_rows(center * center)

    return mean, lax.rsqrt(column_sum(sweep(add, zero_rows(width))) / count + EPSILON)


def pad_chunk(pad_ref, top, at, values):
    for row in range(MAPS):
        start = pl.multiple_of(at * PITCHED, PITCHED) + (8 + top + row * PITCH)
        pad_ref[pl.ds(start, WIDTH), :] = values[row * WIDTH : (row + 1) * WIDTH]


def shift_columns(pad_ref, out_ref):
    rows = out_ref.shape[0]
    for col_off in range(KSIZE):
        start = 8 + col_off - KSIZE // 2
        out_ref[:, col_off * LANES : (col_off + 1) * LANES] = pad_ref[start : start + rows, :].astype(jnp.bfloat16)


def conv_chunk(wide_ref, top, at, weight_of, multiply):
    total = None
    for row_off in range(KSIZE):
        start = pl.multiple_of(at * PITCHED, PITCHED) + (top + (row_off - KSIZE // 2) * PITCH)
        piece = multiply(wide_ref[pl.ds(start, PITCHED), :], weight_of(row_off))
        total = piece if total is None else total + piece
    return jnp.concatenate([total[row * PITCH : row * PITCH + WIDTH] for row in range(MAPS)], axis=0)


def mean_of(own, theirs):
    return (own + theirs) * 0.5


def rows_at(ref, start, rows):
    return ref.at[pl.ds(start, rows), :]


def step_kernel(step, last, split, *refs):
    it = iter(refs)
    take = lambda count: [next(it) for _ in range(count)]
    core_ref = next(it) if last else None
    images_ref, cotangent_ref = take(2)
    packed = step > 0
    own, theirs = (take(2) if packed else take(5)) , (take(2) if packed else take(5))
    held_out = take(2) if packed else []
    outs = take(2) if last else take(2)
    moment_out = next(it)
    norm_moment = next(it)
    own_ref = own[0] if packed else next(it)
    (x_ref, upstream_ref, theirs_ref, param_ref, moment_ref,
     normed_a, normed_b, hidden_b, wide, wide_t, wide_b, pad, pad_b, mixed_e, weight_e, weight_s, weight_f,
     third, grad_sum, grad_third, work, back, weight_t, arrived, left) = take(25)
    held_ref = next(it) if packed else None
    count, width = third.shape
    blocks = width // LANES
    rows_r, rows_s, rows_e = width, weight_s.shape[0], width
    spans = ((0, rows_r), (rows_r, rows_s), (rows_r + rows_s, rows_e))
    bf16 = jnp.bfloat16
    view = lambda ref, part: rows_at(ref, *spans[part])
    pending = {}

    def fetch(name, source, target):
        copy = pltpu.make_async_copy(source, target, arrived.at[len(pending)])
        copy.start()
        pending[name] = copy

    def fetch_part(part):
        fetch(("own", part), own[part], view(own_ref, part))
        fetch(("theirs", part), theirs[part], view(theirs_ref, part))

    def ready(part):
        if not packed:
            pending["own", part].wait()
            pending["theirs", part].wait()
        elif part < 2:
            pending["others" if part else "reduce"].wait()

    fetch("x", images_ref.at[step, 0], x_ref)
    if packed:
        later = rows_s + rows_e
        fetch("reduce", rows_at(theirs[0], 0, rows_r), rows_at(theirs_ref, 0, rows_r))
        fetch("others", rows_at(theirs[0], rows_r, later), rows_at(theirs_ref, rows_r, later))
    else:
        for part in range(3):
            fetch_part(part)
    fetch("upstream", cotangent_ref.at[step, 0], upstream_ref)
    if packed:
        fetch("held", held_out[0], held_ref)
    stores = []

    def store(source, target):
        copy = pltpu.make_async_copy(source, target, left.at[len(stores)])
        copy.start()
        stores.append(copy)

    def settle(start, rows):
        store(rows_at(moment_ref, start, rows), rows_at(moment_out, start, rows))
        if not last:
            store(rows_at(param_ref, start, rows), rows_at(outs[0], start, rows))

    if packed:
        rows_of = lambda ref, low: jnp.concatenate([ref[low + at : low + at + 1, :] for at in range(ref.shape[0] // 2)], axis=1)
        half = own[1].shape[0] // 2
        gains = mean_of(rows_of(own[1], 0), rows_of(theirs[1], 0))
        shifts = mean_of(rows_of(own[1], half), rows_of(theirs[1], half))
    else:
        gains = mean_of(own[3][...], theirs[3][...])
        shifts = mean_of(own[4][...], theirs[4][...])
    gain_a, gain_b, gain_c = gains[:, :LANES], gains[:, LANES : 2 * LANES], gains[:, 2 * LANES :]
    shift_a, shift_b, shift_c = shifts[:, :LANES], shifts[:, LANES : 2 * LANES], shifts[:, 2 * LANES :]

    half_a, half_b = (0.5 * gain_a, 0.5 * shift_a), (0.5 * gain_b, 0.5 * shift_b)

    def mixed(part, start, rows):
        span = pl.ds(spans[part][0] + start, rows)
        return mean_of(own_ref[span, :], theirs_ref[span, :])

    def learn(part, start, rows, moment):
        span = pl.ds(spans[part][0] + start, rows)
        if packed:
            moment = MOMENTUM * held_ref[span, :] + moment
        moment_ref[span, :] = moment
        param_ref[span, :] = mixed(part, start, rows) - LEARN_RATE * moment

    pad[...] = jnp.zeros_like(pad)
    pad_b[...] = jnp.zeros_like(pad_b)
    pending["x"].wait()
    ready(0)
    reduce_w = mixed(0, 0, rows_r).astype(bf16)

    def make_first(at, total):
        values = matmul(x_ref[flat_rows(at), :], reduce_w)
        normed_a[flat_rows(at), :] = values
        return total + fold_rows(values)

    mean, scale_a = statistics(normed_a, sweep(make_first, zero_rows(LANES)))

    def make_hidden_a(at, carry):
        normed = (normed_a[flat_rows(at), :] - mean) * scale_a
        normed_a[flat_rows(at), :] = normed
        pad_chunk(pad, TOP, at, activate_half(normed * half_a[0] + half_a[1]))
        return carry

    sweep(make_hidden_a)
    shift_columns(pad, wide)

    taps = KSIZE * KSIZE
    ready(1)
    for tap in range(taps):
        weights = mixed(1, tap * LANES, LANES).astype(bf16)
        weight_s[tap * LANES : (tap + 1) * LANES, :] = weights
        other = taps - 1 - tap
        weight_f[other * LANES : (other + 1) * LANES, :] = weights.T

    def make_second(at, total):
        values = conv_chunk(wide, TOP, at, lambda row: weight_s[row * SPAN : (row + 1) * SPAN, :], matmul)
        normed_b[flat_rows(at), :] = values
        return total + fold_rows(values)

    mean, scale_b = statistics(normed_b, sweep(make_second, zero_rows(LANES)))

    def make_hidden_b(at, total):
        normed = (normed_b[flat_rows(at), :] - mean) * scale_b
        normed_b[flat_rows(at), :] = normed
        hidden = activate_half(normed * half_b[0] + half_b[1]).astype(bf16)
        hidden_b[flat_rows(at), :] = hidden
        return total + fold_rows(hidden.astype(jnp.float32))

    hidden_mean = column_sum(sweep(make_hidden_b, zero_rows(LANES))) / count

    ready(2)
    mixed_e[...] = mixed(2, 0, rows_e)
    for block in range(blocks):
        weights = mixed_e[pl.ds(block, LANES, stride=blocks), :].astype(bf16)
        weight_e[:, block * LANES : (block + 1) * LANES] = weights
        weight_t[block * LANES : (block + 1) * LANES, :] = weights.T

    rows, rest = [], hidden_mean
    for _ in range(3):
        rows.append(rest.astype(bf16).astype(jnp.float32))
        rest = rest - rows[-1]
    rows = jnp.concatenate(rows + [jnp.zeros((13, LANES), jnp.float32)], axis=0).astype(bf16)
    mean = column_sum(matmul(rows, weight_e[...]))

    def make_third(at, total):
        values = matmul(hidden_b[flat_rows(at), :], weight_e[...]) - mean
        third[flat_rows(at), :] = values
        return total + fold_rows(values * values)

    scale_c = lax.rsqrt(column_sum(sweep(make_third, zero_rows(width))) / count + EPSILON)
    stretch = scale_c * gain_c

    def make_sum(at, totals):
        values = third[flat_rows(at), :]
        half = 0.5 * (values * stretch + (shift_c + x_ref[flat_rows(at), :].astype(jnp.float32)))
        grad = upstream_ref[flat_rows(at), :].astype(jnp.float32) * twice_slope(half)
        grad_sum[flat_rows(at), :] = grad
        return totals[0] + fold_rows(grad * values), totals[1] + fold_rows(grad)

    pending["upstream"].wait()
    totals = sweep(make_sum, (zero_rows(width), zero_rows(width)), False)
    dgain_c, dshift_c = 0.5 * scale_c * column_sum(totals[0]), 0.5 * column_sum(totals[1])
    level, slope, factor = 2.0 * dshift_c / count, 2.0 * scale_c * dgain_c / count, 0.5 * stretch

    def make_back_c(at, totals):
        grad = (grad_sum[flat_rows(at), :] - level - third[flat_rows(at), :] * slope) * factor
        grad = grad.astype(bf16)
        grad_third[flat_rows(at), :] = grad
        normed = normed_b[flat_rows(at), :]
        grad_out = matmul(grad, weight_t[...]) * twice_slope(normed * half_b[0] + half_b[1])
        work[flat_rows(at), :] = grad_out
        return totals[0] + fold_rows(grad_out * normed), totals[1] + fold_rows(grad_out)

    dgain_b, dshift_b = [0.5 * column_sum(total) for total in sweep(make_back_c, (zero_rows(LANES), zero_rows(LANES)))]
    grad = matmul(hidden_b[...].T, grad_third[...])
    for block in range(blocks):
        mixed_e[pl.ds(block, LANES, stride=blocks), :] = grad[:, block * LANES : (block + 1) * LANES]
    if packed:
        pending["held"].wait()
    learn(2, 0, rows_e, mixed_e[...])

    level_b, slope_b, factor_b = 2.0 * dshift_b / count, 2.0 * dgain_b / count, 0.5 * scale_b * gain_b

    def make_back_b(at, carry):
        grad = (work[flat_rows(at), :] - level_b - normed_b[flat_rows(at), :] * slope_b) * factor_b
        pad_chunk(pad_b, TOP_BACK, at, grad)
        return carry

    sweep(make_back_b)
    shift_columns(pad_b, wide_b)

    for at in range(ROWS // LANES):
        wide_t[:, at * LANES : (at + 1) * LANES] = wide[at * LANES : (at + 1) * LANES, :].T

    shifted = [
        wide_b[TOP_BACK - row_off * PITCH : TOP_BACK - row_off * PITCH + ROWS, LANES : 2 * LANES]
        for row_off in range(KSIZE)
    ]
    grad = matmul(wide_t[...], jnp.concatenate(shifted, axis=1))
    for row_off in range(KSIZE):
        learn(1, row_off * SPAN, SPAN, grad[:, row_off * LANES : (row_off + 1) * LANES])
    settle(rows_r, rows_s + rows_e)

    def make_back_a(at, totals):
        grad = conv_chunk(wide_b, TOP_BACK, at, lambda row: weight_f[row * SPAN : (row + 1) * SPAN, :], matmul)
        normed = normed_a[flat_rows(at), :]
        grad_out = grad * twice_slope(normed * half_a[0] + half_a[1])
        work[flat_rows(at), :] = grad_out
        return totals[0] + fold_rows(grad_out * normed), totals[1] + fold_rows(grad_out)

    dgain_a, dshift_a = [0.5 * column_sum(total) for total in sweep(make_back_a, (zero_rows(LANES), zero_rows(LANES)))]
    level_a, slope_a, factor_a = 2.0 * dshift_a / count, 2.0 * dgain_a / count, 0.5 * scale_a * gain_a

    def make_first_grad(at, carry):
        grad = (work[flat_rows(at), :] - level_a - normed_a[flat_rows(at), :] * slope_a) * factor_a
        back[flat_rows(at), :] = grad.astype(bf16)
        return carry

    sweep(make_first_grad)
    grad = matmul(back[...].T, x_ref[...])
    for block in range(blocks):
        learn(0, block * LANES, LANES, grad[:, block * LANES : (block + 1) * LANES].T)
    settle(0, rows_r)
    grad = jnp.concatenate([dgain_a, dgain_b, dgain_c, dshift_a, dshift_b, dshift_c], axis=1)
    norm = jnp.concatenate([gains, shifts], axis=1)
    if packed:
        grad = MOMENTUM * held_out[1][...] + grad
    norm_moment[...] = grad
    norm = norm - LEARN_RATE * grad
    if not last:
        for at in range(norm.shape[1] // LANES):
            outs[1][at : at + 1, :] = norm[:, at * LANES : (at + 1) * LANES]
        for copy in stores:
            copy.wait()
        return

    kept_ref, sent_ref = outs
    is_odd = jnp.full((1, 1), core_ref[0], jnp.int32) == 1
    pairs, piece_s, piece_e, piece_r, piece_n = split
    at_e = round_up(piece_s + 1, 8)
    at_r = at_e + piece_e

    def place(pair, start, low, high):
        rows = low.shape[0]
        kept_ref[pair, start : start + rows, :] = jnp.where(is_odd, high, low)
        sent_ref[pair, start : start + rows, :] = jnp.where(is_odd, low, high)

    for pair in range(pairs):
        for part, rows, start in ((1, piece_s, 0), (2, piece_e, at_e), (0, piece_r, at_r)):
            first = spans[part][0] + 2 * pair * rows
            place(pair, start, param_ref[first : first + rows, :], param_ref[first + rows : first + 2 * rows, :])
        low, high = [
            jnp.concatenate(
                [norm[:, at * piece_n : (at + 1) * piece_n], jnp.zeros((1, LANES - piece_n), jnp.float32)], axis=1
            )
            for at in (2 * pair, 2 * pair + 1)
        ]
        rest = jnp.zeros((at_e - piece_s - 1, LANES), jnp.float32)
        place(pair, piece_s, jnp.concatenate([low, rest]), jnp.concatenate([high, rest]))
    for copy in stores:
        copy.wait()


def fold_kernel(bits, *refs):
    spot_ref, kept_ref = refs[:2]
    came, outs, total = refs[2 : 2 + bits[0]], refs[2 + bits[0] : -1], refs[-1]
    values = kept_ref[...]
    for ref in came:
        values = values + ref[...]
    total[...] = values
    ways = len(outs)
    for hop, out in enumerate(outs):
        for at in range(out.shape[0]):
            out[at] = total[at * ways + jnp.bitwise_xor(spot_ref[0], hop)]


def mean_kernel(replicas, spans, *refs):
    outs = refs[-len(spans) :]
    kept_ref, came = refs[0], refs[1 : -len(spans)]
    values = kept_ref[0]
    for ref in came:
        values = values + ref[0]
    values = values * (1.0 / replicas)
    for (start, rows), out in zip(spans, outs):
        width = out.shape[0] // rows
        for at in range(rows):
            out[at * width : (at + 1) * width] = values[start + at, :width]


def copy_kernel(source, target, sem):
    copy = pltpu.make_async_copy(source, target, sem)
    copy.start()
    copy.wait()


def pack_kernel(spans, *refs):
    source, outs = refs[0], refs[-len(spans) :]
    for (start, rows), out in zip(spans, outs):
        if rows == 0:
            out[...] = refs[1][...].astype(jnp.bfloat16)
            continue

        def lay(at, carry, start=start, out=out):
            base = pl.multiple_of(at * 16, 16)
            for row in range(16):
                values = source[pl.ds(start + base + row, 1), :].astype(jnp.bfloat16)
                out[0:1, pl.ds(pl.multiple_of((base + row) * LANES, LANES), LANES)] = values
            return carry

        lax.fori_loop(0, rows // 16, lay, 0)


def run_kernel(body, name, operands, outs, scratch=(), flops=0, vmem=SMALL_VMEM):
    def parts(entries, is_plain):
        plain = [entry if is_plain(entry) else entry[0] for entry in entries]
        return plain, [pl.BlockSpec(memory_space=pltpu.VMEM if is_plain(entry) else entry[1]) for entry in entries]

    arrays, in_specs = parts(operands, lambda entry: not isinstance(entry, tuple))
    shapes, out_specs = parts(outs, lambda entry: isinstance(entry[0], tuple) and not isinstance(entry[0][0], tuple))
    moved = sum(array.size * array.dtype.itemsize for array in arrays)
    return list(pl.pallas_call(
        body,
        in_specs=in_specs,
        out_specs=out_specs,
        out_shape=[jax.ShapeDtypeStruct(shape, kind) for shape, kind in shapes],
        scratch_shapes=[pltpu.VMEM(*entry) if isinstance(entry, tuple) else entry for entry in scratch],
        compiler_params=pltpu.CompilerParams(vmem_limit_bytes=vmem),
        cost_estimate=pl.CostEstimate(flops=flops, bytes_accessed=moved, transcendentals=0),
        name=name,
    )(*arrays))


def in_hbm(entry):
    return entry, pltpu.HBM


def in_smem(value):
    return value.astype(jnp.int32).reshape(1), pltpu.SMEM


def swap_all(bit, values):
    return [partner_2(member, "dp", bit) for member in values]


def exchange(spot, first_bit, ways, sends):
    replicas = lax.axis_size("dp")
    return [
        lax.ppermute(sent, "dp", [(at, at ^ (hop << first_bit)) for at in range(replicas)])
        for hop, sent in zip(range(1, ways), sends)
    ]


def scatter_mean(kept, sent, split, beside):
    f32 = jnp.float32
    replicas = lax.axis_size("dp")
    levels = replicas.bit_length() - 1
    place = lax.axis_index("dp")
    pairs, piece_s, piece_e, piece_r, piece_n = split
    rows = kept.shape[1]
    came = exchange(place, 0, 2, [sent])
    (kept,) = run_kernel(
        copy_kernel, "copy", [in_hbm(kept)], [(kept.shape, f32)], [pltpu.SemaphoreType.DMA(())]
    )
    came, kept = lax.optimization_barrier((came, kept))
    left, low, done = pairs, 1, []
    while left > 1:
        width = 2 if low == 1 and levels > 2 else 1
        ways = 1 << width
        spot = in_smem((place >> low) % ways)
        kept, *sends = run_kernel(
            functools.partial(fold_kernel, (len(came),)), "fold", [spot, kept] + came,
            [((left // ways, rows, LANES), f32)] * ways, [((left, rows, LANES), f32)],
        )
        came = exchange(place, low, ways, sends)
        if beside:
            work, *beside = beside
            came, ready = lax.optimization_barrier((came, work()))
            done.append(ready)
        left, low = left // ways, low + width
    at_e = round_up(piece_s + 1, 8)
    spans = ((at_e + piece_e, piece_r), (0, piece_s), (at_e, piece_e), (piece_s, 1))
    sizes = [(rows_of * LANES,) for _, rows_of in spans[:3]] + [(piece_n,)]
    mean = run_kernel(
        functools.partial(mean_kernel, replicas, spans), "mean", [kept] + came, [(size, f32) for size in sizes]
    )
    return done + [work() for work in beside], mean


def scatter_mean_any(arrays):
    replicas = lax.axis_size("dp")
    tables = [member.reshape(replicas, -1) for member in arrays]
    pieces = lax.all_to_all(jnp.concatenate(tables, axis=1), "dp", 0, 0, tiled=True)
    mean = jnp.sum(pieces, axis=0) / replicas
    bounds = [sum(table.shape[1] for table in tables[:at]) for at in range(len(tables) + 1)]
    return tuple(mean[low:high] for low, high in zip(bounds[:-1], bounds[1:]))


def shards(images, cotangent, w_reduce, w_spatial, w_expand, norm_gain, norm_bias, round_index):
    f32, bf16 = jnp.float32, jnp.bfloat16
    replicas = lax.axis_size("dp")
    levels = replicas.bit_length() - 1
    steps, _, pixels, in_ch = images.shape
    weights = [member.reshape(-1, LANES) for member in (w_reduce, w_spatial, w_expand)]
    sizes = [(member.shape, f32) for member in weights]
    rows_r, rows_s, rows_e = (member.shape[0] for member in weights)
    rows = rows_r + rows_s + rows_e
    norm_size = 2 * norm_gain.size
    flat_map = ((pixels, LANES), f32)
    wide_map = ((pixels, in_ch), f32)
    whole = ((rows, LANES), f32)
    norm_rows = ((norm_size // LANES, LANES), f32)
    half_map = ((pixels, in_ch), bf16)
    scratch = [
        half_map, half_map, whole, whole, whole,
        flat_map, flat_map, ((pixels, LANES), bf16), ((ROWS, SPAN), bf16), ((SPAN, ROWS), bf16),
        ((ROWS_BACK, SPAN), bf16), ((ROWS + 16, LANES), f32), ((ROWS_BACK + 16, LANES), f32),
        sizes[2], ((LANES, in_ch), bf16), ((rows_s, LANES), bf16), ((rows_s, LANES), bf16),
        wide_map, wide_map, half_map, flat_map, ((pixels, LANES), bf16), ((in_ch, LANES), bf16),
        pltpu.SemaphoreType.DMA((8,)), pltpu.SemaphoreType.DMA((4,)),
    ]
    flops = 6 * pixels * LANES * (2 * in_ch + rows_s)
    fine = replicas > 1 and all(size[0][0] % replicas == 0 for size in sizes)
    split = (replicas // 2, rows_s // replicas, rows_e // replicas, rows_r // replicas, norm_size // replicas)
    half = ((split[0], round_up(split[1] + 1, 8) + split[2] + split[3], LANES), f32)
    params = [weights[1], weights[0], weights[2], norm_gain, norm_bias]
    moments = []
    for step in range(steps):
        branches = [functools.partial(swap_all, bit) for bit in range(levels)]
        theirs = list(lax.switch((round_index[0] + step) % levels, branches, params))
        if step == 0:
            sides = [[in_hbm(side[at]) for at in (1, 0, 2)] + side[3:] for side in (params, theirs)]
        else:
            sides = [params, [in_hbm(theirs[0]), theirs[1]]]
        operands = [in_hbm(images), in_hbm(cotangent)] + sides[0] + sides[1]
        operands += [in_hbm(member) for member in moments[:1]] + moments[1:]
        moment_outs = [in_hbm(whole), ((1, norm_size), f32)]
        scratch_of = scratch + [whole] if step else [whole] + scratch
        if step == steps - 1 and fine:
            core = in_smem(lax.axis_index("dp") % 2)
            kept, sent, *moments = run_kernel(
                functools.partial(step_kernel, step, True, split), "last_step", [core] + operands,
                [half, half] + moment_outs, scratch_of, flops, VMEM_BYTES,
            )
        else:
            *params, moment, norm_moment = run_kernel(
                functools.partial(step_kernel, step, False, None), "step", operands,
                [in_hbm(whole), norm_rows] + moment_outs, scratch_of, flops, VMEM_BYTES,
            )
            moments = [moment, norm_moment]
    def pack(sources, *spans):
        return run_kernel(
            functools.partial(pack_kernel, spans), "pack", sources,
            [((1, span * LANES if span else norm_size), bf16) for _, span in spans],
        )

    span_r, span_s, span_e = (0, rows_r), (rows_r, rows_s), (rows_r + rows_s, rows_e)
    if fine:
        beside = [
            functools.partial(pack, moments[:1], span_r, span_s), functools.partial(pack, moments, span_e, (0, 0))
        ]
        (first, second), averaged = scatter_mean(kept, sent, split, beside)
        out = first + second
    else:
        flat = [params[0][low:high].reshape(-1) for low, high in ((0, rows_r), (rows_r, rows_r + rows_s), (rows_r + rows_s, rows))]
        out, averaged = pack(moments, span_r, span_s, span_e, (0, 0)), scatter_mean_any(flat + [params[1].reshape(-1)])
    return tuple(averaged) + tuple(out)


def solution(mesh):
    in_specs = (
        P(None, "dp", None, None),
        P(None, "dp", None, None),
        P("dp", None),
        P("dp", None),
        P("dp", None),
        P("dp", None),
        P("dp", None),
        P(),
    )
    out_specs = (
        P("dp"),
        P("dp"),
        P("dp"),
        P("dp"),
        P("dp", None),
        P("dp", None),
        P("dp", None),
        P("dp", None),
    )
    return jax.shard_map(shards, mesh=mesh, in_specs=in_specs, out_specs=out_specs, check_vma=False)
```

profile of v0, /device:TPU:0, one launch (start us, length us, event | category | flops | bytes accessed | tf_op | source)
XLA Modules:
  0.0 99.0 jit_solution(5994034372505328511)
XLA Ops:
  1.3 53.2 %conditional.2 = (f32[1152,128]{1,0:T(8,128)}, f32[512,128]{1,0:T(8,128)}, f32[512,128]{1,0:T(8,128)}, f32[1,768]{1,0:T(1,128)}, f32[1,768]{1,0:T(1,128)}) conditional(s32[]{:T(128)} %clamp.6, (f32[1152,128]{1,0:T(8,128)}, f32[512,128]{1,0:T(8,128)}, f32[512,128]{1,0:T(8,128)}, f32[1,768]{1,0:T(1,128)}, ...), branch_computations={%region_0.1_spmd, %region_1.2_spmd, %region_2.3_spmd, %region_3.4_... | conditional | bytes 4481264 | solution.py:559
  1.4 4.1 %collective-permute-start.20 = (f32[1152,128]{1,0:T(8,128)}, f32[1152,128]{1,0:T(8,128)}, u32[]{:S(2)}, u32[]{:S(2)}) collective-permute-start(f32[1152,128]{1,0:T(8,128)} %get-tuple-element.90), channel_id=1, source_target_pairs={{0,16},{1,17},{2,18},{3,19},{4,20},{5,21},{6,22},{7,23},{8,24},{9,... | collective-permute-start | bytes 1769480 | tf_op jit(solution)/shard_map/cond/branch_4_fun/ppermute | solution.py:31
  5.5 0.1 collective-permute-start.21
  5.5 2.8 %collective-permute-start.22 = (f32[512,128]{1,0:T(8,128)}, f32[512,128]{1,0:T(8,128)}, u32[]{:S(2)}, u32[]{:S(2)}) collective-permute-start(f32[512,128]{1,0:T(8,128)} %get-tuple-element.92), channel_id=1, source_target_pairs={{0,16},{1,17},{2,18},{3,19},{4,20},{5,21},{6,22},{7,23},{8,24},{9,... | collective-permute-start | bytes 786440 | tf_op jit(solution)/shard_map/cond/branch_4_fun/ppermute | solution.py:31
  8.4 0.1 collective-permute-start.23
  8.5 2.8 %collective-permute-start.24 = (f32[1,768]{1,0:T(1,128)}, f32[1,768]{1,0:T(1,128)}, u32[]{:S(2)}, u32[]{:S(2)}) collective-permute-start(f32[1,768]{1,0:T(1,128)} %get-tuple-element.94), channel_id=1, source_target_pairs={{0,16},{1,17},{2,18},{3,19},{4,20},{5,21},{6,22},{7,23},{8,24},{9,... | collective-permute-start | bytes 9224 | tf_op jit(solution)/shard_map/cond/branch_4_fun/ppermute | solution.py:31
  11.3 43.1 %collective-permute-done.23 = f32[1,768]{1,0:T(1,128)} collective-permute-done((f32[1,768]{1,0:T(1,128)}, f32[1,768]{1,0:T(1,128)}, u32[]{:S(2)}, u32[]{:S(2)}) %collective-permute-start.23) | collective-permute-done | bytes 3104 | tf_op jit(solution)/shard_map/cond/branch_4_fun/ppermute | solution.py:31
  54.4 0.0 collective-permute-done.24
  54.5 0.0 collective-permute-done.21
  54.5 0.0 collective-permute-done.22
  54.5 0.0 collective-permute-done.20
  54.5 9.1 %step.1 = (f32[2176,128]{1,0:T(8,128)S(1)}, f32[12,128]{1,0:T(8,128)S(1)}, f32[2176,128]{1,0:T(8,128)}, f32[1,1536]{1,0:T(1,128)}) custom-call(bf16[2,1,784,512]{3,2,1,0:T(8,128)(2,1)} %refs_1_.3, bf16[2,1,784,512]{3,2,1,0:T(8,128)(2,1)} %refs_2_.1, f32[512,128]{1,0:T(8,128)} %bitcast.20, f32[1152,128]{1,0:T(8,128)} %bitcast.14, f32[512,128]{1,0:T(8,128)} %bitcast.26, ...), custom_call_target="tpu_custom_call" | custom-call | flops 1310195712 | bytes 5451776 | tf_op jit(solution)/shard_map/step/pallas_call | solution.py:451
  63.6 3.0 %conditional.3 = (f32[2176,128]{1,0:T(8,128)}, f32[12,128]{1,0:T(8,128)}) conditional(s32[]{:T(128)} %clamp.7, (f32[2176,128]{1,0:T(8,128)S(1)}, f32[12,128]{1,0:T(8,128)S(1)}) %tuple.52, (f32[2176,128]{1,0:T(8,128)S(1)}, f32[12,128]{1,0:T(8,128)S(1)}) %tuple.52, (f32[2176,128]{1,0:T(8,128)S(1)}, ...), branch_computations={%region_5.6_spmd, %region_6.7_spmd, %region_7.8_spmd, %region_8.9_... | conditional | bytes 4481120 | solution.py:559
  63.7 0.1 collective-permute-start.25
  63.7 0.5 collective-permute-start.26
  64.2 2.4 %collective-permute-done.26 = f32[12,128]{1,0:T(8,128)} collective-permute-done((f32[12,128]{1,0:T(8,128)S(1)}, f32[12,128]{1,0:T(8,128)}, u32[]{:S(2)}, u32[]{:S(2)}) %collective-permute-start.26) | collective-permute-done | bytes 6176 | tf_op jit(solution)/shard_map/cond/branch_0_fun/ppermute | solution.py:31
  66.6 0.0 collective-permute-done.25
  66.6 9.6 %last_step.1 = (f32[16,72,128]{2,1,0:T(8,128)}, f32[16,72,128]{2,1,0:T(8,128)}, f32[2176,128]{1,0:T(8,128)}, f32[1,1536]{1,0:T(1,128)}) custom-call(s32[1]{0:T(128)} %bitcast.3.refs_0_, bf16[2,1,784,512]{3,2,1,0:T(8,128)(2,1)} %refs_1_.3, bf16[2,1,784,512]{3,2,1,0:T(8,128)(2,1)} %refs_2_.1, f32[2176,128]{1,0:T(8,128)S(1)} %get-tuple-element.159.refs_3_, ...), custom_call_target="tpu_custom_call" | custom-call | flops 1310195712 | bytes 6572036 | tf_op jit(solution)/shard_map/last_step/pallas_call | solution.py:451
  76.2 0.2 collective-permute-start.35
  76.4 0.0 copy-start.1
  76.4 1.1 %copy-done.1 = f32[16,72,128]{2,1,0:T(8,128)S(1)} copy-done((f32[16,72,128]{2,1,0:T(8,128)S(1)}, f32[16,72,128]{2,1,0:T(8,128)}, u32[]{:S(2)}) %copy-start.1) | copy-done | bytes 589848
  77.5 0.0 copy-start
  77.5 0.1 copy.53.refs_1_
  77.6 0.9 collective-permute-done.35.refs_2_
  78.5 0.1 fold.3
  78.6 0.0 copy-start.2
  78.6 1.6 %collective-permute-start.36 = (f32[4,72,128]{2,1,0:T(8,128)S(1)}, f32[4,72,128]{2,1,0:T(8,128)S(1)}, u32[]{:S(2)}, u32[]{:S(2)}) collective-permute-start(f32[4,72,128]{2,1,0:T(8,128)S(1)} %get-tuple-element.170), channel_id=1, source_target_pairs={{0,2},{1,3},{2,0},{3,1},{4,6},{5,7},{6,4},{7,5},{8,10},{9,11},{10,... | collective-permute-start | bytes 442376 | tf_op jit(solution)/shard_map/ppermute | solution.py:478
  80.2 1.5 %collective-permute-start.37 = (f32[4,72,128]{2,1,0:T(8,128)S(1)}, f32[4,72,128]{2,1,0:T(8,128)S(1)}, u32[]{:S(2)}, u32[]{:S(2)}) collective-permute-start(f32[4,72,128]{2,1,0:T(8,128)S(1)} %get-tuple-element.171), channel_id=1, source_target_pairs={{0,4},{1,5},{2,6},{3,7},{4,0},{5,1},{6,2},{7,3},{8,12},{9,13},{10,... | collective-permute-start | bytes 442376 | tf_op jit(solution)/shard_map/ppermute | solution.py:478
  81.7 0.4 collective-permute-start.38
  82.2 0.0 copy-done
  82.2 5.1 %pack.2 = (bf16[1,65536]{1,0:T(2,128)(2,1)}, bf16[1,147456]{1,0:T(2,128)(2,1)}) custom-call(f32[2176,128]{1,0:T(8,128)S(1)} %copy-done), custom_call_target="tpu_custom_call" | custom-call | bytes 1114112 | tf_op jit(solution)/shard_map/pack/pallas_call | solution.py:451
  87.3 0.0 collective-permute-done.36.refs_2_
  87.3 1.7 %collective-permute-done.37.refs_3_ = f32[4,72,128]{2,1,0:T(8,128)S(1)} collective-permute-done((f32[4,72,128]{2,1,0:T(8,128)S(1)}, f32[4,72,128]{2,1,0:T(8,128)S(1)}, u32[]{:S(2)}, u32[]{:S(2)}) %collective-permute-start.37) | collective-permute-done | bytes 147488 | tf_op jit(solution)/shard_map/ppermute | solution.py:478
  89.0 0.0 collective-permute-done.38.refs_4_
  89.0 0.7 collective-permute-start.39
  89.7 0.0 copy-done.2
  89.7 2.1 %pack.3 = (bf16[1,65536]{1,0:T(2,128)(2,1)}, bf16[1,1536]{1,0:T(2,128)(2,1)}) custom-call(f32[2176,128]{1,0:T(8,128)S(1)} %copy-done, f32[1,1536]{1,0:T(1,128)S(1)} %copy-done.2), custom_call_target="tpu_custom_call" | custom-call | bytes 1120256 | tf_op jit(solution)/shard_map/pack/pallas_call | solution.py:451
  91.8 1.7 %collective-permute-done.39.refs_2_ = f32[2,72,128]{2,1,0:T(8,128)S(1)} collective-permute-done((f32[2,72,128]{2,1,0:T(8,128)S(1)}, f32[2,72,128]{2,1,0:T(8,128)S(1)}, u32[]{:S(2)}, u32[]{:S(2)}) %collective-permute-start.39) | collective-permute-done | bytes 73760 | tf_op jit(solution)/shard_map/ppermute | solution.py:478
  93.5 2.1 %collective-permute-start.40 = (f32[1,72,128]{2,1,0:T(8,128)S(1)}, f32[1,72,128]{2,1,0:T(8,128)S(1)}, u32[]{:S(2)}, u32[]{:S(2)}) collective-permute-start(f32[1,72,128]{2,1,0:T(8,128)S(1)} %get-tuple-element.186), channel_id=1, source_target_pairs={{0,16},{1,17},{2,18},{3,19},{4,20},{5,21},{6,22},{7,23},{8,24},{9,... | collective-permute-start | bytes 110600 | tf_op jit(solution)/shard_map/ppermute | solution.py:478
  95.6 2.8 %collective-permute-done.40.refs_1_ = f32[1,72,128]{2,1,0:T(8,128)S(1)} collective-permute-done((f32[1,72,128]{2,1,0:T(8,128)S(1)}, f32[1,72,128]{2,1,0:T(8,128)S(1)}, u32[]{:S(2)}, u32[]{:S(2)}) %collective-permute-start.40) | collective-permute-done | bytes 36896 | tf_op jit(solution)/shard_map/ppermute | solution.py:478
  98.4 0.6 mean.1
  (2 shorter events, 0.1 us)
Async XLA Ops:
  1.4 53.1 %collective-permute-start.20 = (f32[1152,128]{1,0:T(8,128)}, f32[1152,128]{1,0:T(8,128)}, u32[]{:S(2)}, u32[]{:S(2)}) collective-permute-start(f32[1152,128]{1,0:T(8,128)} %get-tuple-element.90), channel_id=1, source_target_pairs={{0,16},{1,17},{2,18},{3,19},{4,20},{5,21},{6,22},{7,23},{8,24},{9,... | collective-permute-start | bytes 1769480 | tf_op jit(solution)/shard_map/cond/branch_4_fun/ppermute | solution.py:31
  5.5 49.0 %collective-permute-start.21 = (f32[512,128]{1,0:T(8,128)}, f32[512,128]{1,0:T(8,128)}, u32[]{:S(2)}, u32[]{:S(2)}) collective-permute-start(f32[512,128]{1,0:T(8,128)} %get-tuple-element.91), channel_id=1, source_target_pairs={{0,16},{1,17},{2,18},{3,19},{4,20},{5,21},{6,22},{7,23},{8,24},{9,... | collective-permute-start | bytes 786440 | tf_op jit(solution)/shard_map/cond/branch_4_fun/ppermute | solution.py:31
  5.5 48.9 %collective-permute-start.22 = (f32[512,128]{1,0:T(8,128)}, f32[512,128]{1,0:T(8,128)}, u32[]{:S(2)}, u32[]{:S(2)}) collective-permute-start(f32[512,128]{1,0:T(8,128)} %get-tuple-element.92), channel_id=1, source_target_pairs={{0,16},{1,17},{2,18},{3,19},{4,20},{5,21},{6,22},{7,23},{8,24},{9,... | collective-permute-start | bytes 786440 | tf_op jit(solution)/shard_map/cond/branch_4_fun/ppermute | solution.py:31
  8.4 46.1 %collective-permute-start.23 = (f32[1,768]{1,0:T(1,128)}, f32[1,768]{1,0:T(1,128)}, u32[]{:S(2)}, u32[]{:S(2)}) collective-permute-start(f32[1,768]{1,0:T(1,128)} %get-tuple-element.93), channel_id=1, source_target_pairs={{0,16},{1,17},{2,18},{3,19},{4,20},{5,21},{6,22},{7,23},{8,24},{9,... | collective-permute-start | bytes 9224 | tf_op jit(solution)/shard_map/cond/branch_4_fun/ppermute | solution.py:31
  8.5 46.0 %collective-permute-start.24 = (f32[1,768]{1,0:T(1,128)}, f32[1,768]{1,0:T(1,128)}, u32[]{:S(2)}, u32[]{:S(2)}) collective-permute-start(f32[1,768]{1,0:T(1,128)} %get-tuple-element.94), channel_id=1, source_target_pairs={{0,16},{1,17},{2,18},{3,19},{4,20},{5,21},{6,22},{7,23},{8,24},{9,... | collective-permute-start | bytes 9224 | tf_op jit(solution)/shard_map/cond/branch_4_fun/ppermute | solution.py:31
  63.7 3.0 %collective-permute-start.25 = (f32[2176,128]{1,0:T(8,128)S(1)}, f32[2176,128]{1,0:T(8,128)}, u32[]{:S(2)}, u32[]{:S(2)}) collective-permute-start(f32[2176,128]{1,0:T(8,128)S(1)} %get-tuple-element.95), channel_id=1, source_target_pairs={{0,1},{1,0},{2,3},{3,2},{4,5},{5,4},{6,7},{7,6},{8,9},{9,8},{10,11... | collective-permute-start | bytes 3342344 | tf_op jit(solution)/shard_map/cond/branch_0_fun/ppermute | solution.py:31
  63.7 2.9 %collective-permute-start.26 = (f32[12,128]{1,0:T(8,128)S(1)}, f32[12,128]{1,0:T(8,128)}, u32[]{:S(2)}, u32[]{:S(2)}) collective-permute-start(f32[12,128]{1,0:T(8,128)S(1)} %get-tuple-element.96), channel_id=1, source_target_pairs={{0,1},{1,0},{2,3},{3,2},{4,5},{5,4},{6,7},{7,6},{8,9},{9,8},{10,11... | collective-permute-start | bytes 18440 | tf_op jit(solution)/shard_map/cond/branch_0_fun/ppermute | solution.py:31
  76.2 2.3 %collective-permute-start.35 = (f32[16,72,128]{2,1,0:T(8,128)}, f32[16,72,128]{2,1,0:T(8,128)S(1)}, u32[]{:S(2)}, u32[]{:S(2)}) collective-permute-start(f32[16,72,128]{2,1,0:T(8,128)} %get-tuple-element.165), channel_id=1, source_target_pairs={{0,1},{1,0},{2,3},{3,2},{4,5},{5,4},{6,7},{7,6},{8,9},{9,8},{10,11... | collective-permute-start | bytes 1769480 | tf_op jit(solution)/shard_map/ppermute | solution.py:478
  76.4 1.1 %copy-start.1 = (f32[16,72,128]{2,1,0:T(8,128)S(1)}, f32[16,72,128]{2,1,0:T(8,128)}, u32[]{:S(2)}) copy-start(f32[16,72,128]{2,1,0:T(8,128)} %get-tuple-element.166.source) | copy-start | bytes 1769476
  77.5 4.7 %copy-start = (f32[2176,128]{1,0:T(8,128)S(1)}, f32[2176,128]{1,0:T(8,128)}, u32[]{:S(2)}) copy-start(f32[2176,128]{1,0:T(8,128)} %get-tuple-element.173.refs_0_) | copy-start | bytes 3342340
  78.6 11.1 %copy-start.2 = (f32[1,1536]{1,0:T(1,128)S(1)}, f32[1,1536]{1,0:T(1,128)}, u32[]{:S(2)}) copy-start(f32[1,1536]{1,0:T(1,128)} %get-tuple-element.181.refs_1_) | copy-start | bytes 18436
  78.6 8.7 %collective-permute-start.36 = (f32[4,72,128]{2,1,0:T(8,128)S(1)}, f32[4,72,128]{2,1,0:T(8,128)S(1)}, u32[]{:S(2)}, u32[]{:S(2)}) collective-permute-start(f32[4,72,128]{2,1,0:T(8,128)S(1)} %get-tuple-element.170), channel_id=1, source_target_pairs={{0,2},{1,3},{2,0},{3,1},{4,6},{5,7},{6,4},{7,5},{8,10},{9,11},{10,... | collective-permute-start | bytes 442376 | tf_op jit(solution)/shard_map/ppermute | solution.py:478
  80.2 8.8 %collective-permute-start.37 = (f32[4,72,128]{2,1,0:T(8,128)S(1)}, f32[4,72,128]{2,1,0:T(8,128)S(1)}, u32[]{:S(2)}, u32[]{:S(2)}) collective-permute-start(f32[4,72,128]{2,1,0:T(8,128)S(1)} %get-tuple-element.171), channel_id=1, source_target_pairs={{0,4},{1,5},{2,6},{3,7},{4,0},{5,1},{6,2},{7,3},{8,12},{9,13},{10,... | collective-permute-start | bytes 442376 | tf_op jit(solution)/shard_map/ppermute | solution.py:478
  81.7 7.3 %collective-permute-start.38 = (f32[4,72,128]{2,1,0:T(8,128)S(1)}, f32[4,72,128]{2,1,0:T(8,128)S(1)}, u32[]{:S(2)}, u32[]{:S(2)}) collective-permute-start(f32[4,72,128]{2,1,0:T(8,128)S(1)} %get-tuple-element.172), channel_id=1, source_target_pairs={{0,6},{1,7},{2,4},{3,5},{4,2},{5,3},{6,0},{7,1},{8,14},{9,15},{10,... | collective-permute-start | bytes 442376 | tf_op jit(solution)/shard_map/ppermute | solution.py:478
  89.0 4.4 %collective-permute-start.39 = (f32[2,72,128]{2,1,0:T(8,128)S(1)}, f32[2,72,128]{2,1,0:T(8,128)S(1)}, u32[]{:S(2)}, u32[]{:S(2)}) collective-permute-start(f32[2,72,128]{2,1,0:T(8,128)S(1)} %get-tuple-element.180), channel_id=1, source_target_pairs={{0,8},{1,9},{2,10},{3,11},{4,12},{5,13},{6,14},{7,15},{8,0},{9,1},... | collective-permute-start | bytes 221192 | tf_op jit(solution)/shard_map/ppermute | solution.py:478
  93.5 4.9 %collective-permute-start.40 = (f32[1,72,128]{2,1,0:T(8,128)S(1)}, f32[1,72,128]{2,1,0:T(8,128)S(1)}, u32[]{:S(2)}, u32[]{:S(2)}) collective-permute-start(f32[1,72,128]{2,1,0:T(8,128)S(1)} %get-tuple-element.186), channel_id=1, source_target_pairs={{0,16},{1,17},{2,18},{3,19},{4,20},{5,21},{6,22},{7,23},{8,24},{9,... | collective-permute-start | bytes 110600 | tf_op jit(solution)/shard_map/ppermute | solution.py:478
where the time goes:
time: 99.4 us; the launch traced here: 99 us
  waiting for transfers between devices  52.6 us (53%)
  Pallas kernels  26.9 us (27%)
  starting transfers between devices  17.1 us (17%)
  between operations  1.39 us (1%)
  local copies, waits for them, and re-layouts  1.07 us (1%)
    ppermute x7, waiting for transfers between devices, partner_2(): return lax.ppermute(value, axis, pairs)  45.6 us
    pallas_call x9, Pallas kernels, run_kernel(): pl.pallas_call(body, in_specs=in_specs, out_specs=out_specs, out_shape=[j...  26.9 us
    ppermute x7, starting transfers between devices, partner_2(): return lax.ppermute(value, axis, pairs)  10.5 us
    ppermute x6, waiting for transfers between devices, exchange(): lax.ppermute(sent, 'dp', [(at, at ^ hop << first_bit) for at in range(rep...  7.03 us
    ppermute x6, starting transfers between devices, exchange(): lax.ppermute(sent, 'dp', [(at, at ^ hop << first_bit) for at in range(rep...  6.54 us
  transfers between devices with their start and end apart: 13, of which 6 were waited for; matrix products, arithmetic and copies ran while one was open for 0% of the time, Pallas kernels for 7%

commit v1 on v0

--- a/solution.py
+++ b/solution.py
@@ -53,6 +53,7 @@
 
 
 MAPS = 4
+THIN = 16
 FLAT = MAPS * WIDTH
 PITCHED = MAPS * PITCH
 CHUNKS = HEIGHT // MAPS
@@ -281,11 +282,15 @@
     stretch = scale_c * gain_c
 
     def make_sum(at, totals):
-        values = third[flat_rows(at), :]
-        half = 0.5 * (values * stretch + (shift_c + x_ref[flat_rows(at), :].astype(jnp.float32)))
-        grad = upstream_ref[flat_rows(at), :].astype(jnp.float32) * twice_slope(half)
-        grad_sum[flat_rows(at), :] = grad
-        return totals[0] + fold_rows(grad * values), totals[1] + fold_rows(grad)
+        size = THIN if packed else FLAT
+        for piece in range(FLAT // size):
+            rows = pl.ds(pl.multiple_of(at * FLAT + piece * size, size), size)
+            values = third[rows, :]
+            half = 0.5 * (values * stretch + (shift_c + x_ref[rows, :].astype(jnp.float32)))
+            grad = upstream_ref[rows, :].astype(jnp.float32) * twice_slope(half)
+            grad_sum[rows, :] = grad
+            totals = totals[0] + fold_rows(grad * values), totals[1] + fold_rows(grad)
+        return totals
 
     pending["upstream"].wait()
     totals = sweep(make_sum, (zero_rows(width), zero_rows(width)), False)
@@ -293,11 +298,13 @@
     level, slope, factor = 2.0 * dshift_c / count, 2.0 * scale_c * dgain_c / count, 0.5 * stretch
 
     def make_back_c(at, totals):
-        grad = (grad_sum[flat_rows(at), :] - level - third[flat_rows(at), :] * slope) * factor
-        grad = grad.astype(bf16)
-        grad_third[flat_rows(at), :] = grad
+        size = FLAT if packed else THIN
+        for piece in range(FLAT // size):
+            rows = pl.ds(pl.multiple_of(at * FLAT + piece * size, size), size)
+            grad = (grad_sum[rows, :] - level - third[rows, :] * slope) * factor
+            grad_third[rows, :] = grad.astype(bf16)
         normed = normed_b[flat_rows(at), :]
-        grad_out = matmul(grad, weight_t[...]) * twice_slope(normed * half_b[0] + half_b[1])
+        grad_out = matmul(grad_third[flat_rows(at), :], weight_t[...]) * twice_slope(normed * half_b[0] + half_b[1])
         work[flat_rows(at), :] = grad_out
         return totals[0] + fold_rows(grad_out * normed), totals[1] + fold_rows(grad_out)
 

time: 99.4 us -> 97.3 us (0.979)
  waiting for transfers between devices: 52.6 us -> 50.4 us
    ppermute x6, waiting for transfers between devices: 7.03 us -> 5.46 us  [exchange(): lax.ppermute(sent, 'dp', [(at, at ^ hop << first_bit) for at in range(rep...]
    ppermute x6, starting transfers between devices: 6.54 us -> 7.92 us  [exchange(): lax.ppermute(sent, 'dp', [(at, at ^ hop << first_bit) for at in range(rep...]
    ppermute x7, starting transfers between devices: 10.5 us -> 9.17 us  [partner_2(): return lax.ppermute(value, axis, pairs)]
  transfers between devices with their start and end apart: 13 -> 13, of which waited for: 6 -> 6; matrix products, arithmetic and copies ran while one was open for 0% -> 0% of each run, Pallas kernels for 7% -> 8%
where the time goes in v1:
time: 97.3 us; the launch traced here: 97 us
  waiting for transfers between devices  50.4 us (52%)
  Pallas kernels  26.9 us (28%)
  starting transfers between devices  17.1 us (18%)
  between operations  1.42 us (1%)
  local copies, waits for them, and re-layouts  1.07 us (1%)
    ppermute x7, waiting for transfers between devices, partner_2(): return lax.ppermute(value, axis, pairs)  45 us
    pallas_call x9, Pallas kernels, run_kernel(): pl.pallas_call(body, in_specs=in_specs, out_specs=out_specs, out_shape=[j...  26.9 us
    ppermute x7, starting transfers between devices, partner_2(): return lax.ppermute(value, axis, pairs)  9.17 us
    ppermute x6, starting transfers between devices, exchange(): lax.ppermute(sent, 'dp', [(at, at ^ hop << first_bit) for at in range(rep...  7.92 us
    ppermute x6, waiting for transfers between devices, exchange(): lax.ppermute(sent, 'dp', [(at, at ^ hop << first_bit) for at in range(rep...  5.46 us
  transfers between devices with their start and end apart: 13, of which 6 were waited for; matrix products, arithmetic and copies ran while one was open for 0% of the time, Pallas kernels for 8%

profile of v1, /device:TPU:0, one launch (start us, length us, event | category | flops | bytes accessed | tf_op | source)
XLA Modules:
  0.0 97.0 jit_solution(6940379356816128555)
XLA Ops:
  1.3 28.1 %conditional.2 = (f32[1152,128]{1,0:T(8,128)}, f32[512,128]{1,0:T(8,128)}, f32[512,128]{1,0:T(8,128)}, f32[1,768]{1,0:T(1,128)}, f32[1,768]{1,0:T(1,128)}) conditional(s32[]{:T(128)} %clamp.6, (f32[1152,128]{1,0:T(8,128)}, f32[512,128]{1,0:T(8,128)}, f32[512,128]{1,0:T(8,128)}, f32[1,768]{1,0:T(1,128)}, ...), branch_computations={%region_0.1_spmd, %region_1.2_spmd, %region_2.3_spmd, %region_3.4_... | conditional | bytes 4481264 | solution.py:566
  1.3 3.0 %collective-permute-start.10 = (f32[1152,128]{1,0:T(8,128)}, f32[1152,128]{1,0:T(8,128)}, u32[]{:S(2)}, u32[]{:S(2)}) collective-permute-start(f32[1152,128]{1,0:T(8,128)} %get-tuple-element.80), channel_id=1, source_target_pairs={{0,4},{1,5},{2,6},{3,7},{4,0},{5,1},{6,2},{7,3},{8,12},{9,13},{10,... | collective-permute-start | bytes 1769480 | tf_op jit(solution)/shard_map/cond/branch_2_fun/ppermute | solution.py:31
  4.4 0.1 collective-permute-start.11
  4.5 1.9 %collective-permute-start.12 = (f32[512,128]{1,0:T(8,128)}, f32[512,128]{1,0:T(8,128)}, u32[]{:S(2)}, u32[]{:S(2)}) collective-permute-start(f32[512,128]{1,0:T(8,128)} %get-tuple-element.82), channel_id=1, source_target_pairs={{0,4},{1,5},{2,6},{3,7},{4,0},{5,1},{6,2},{7,3},{8,12},{9,13},{10,... | collective-permute-start | bytes 786440 | tf_op jit(solution)/shard_map/cond/branch_2_fun/ppermute | solution.py:31
  6.4 0.1 collective-permute-start.13
  6.5 1.9 %collective-permute-start.14 = (f32[1,768]{1,0:T(1,128)}, f32[1,768]{1,0:T(1,128)}, u32[]{:S(2)}, u32[]{:S(2)}) collective-permute-start(f32[1,768]{1,0:T(1,128)} %get-tuple-element.84), channel_id=1, source_target_pairs={{0,4},{1,5},{2,6},{3,7},{4,0},{5,1},{6,2},{7,3},{8,12},{9,13},{10,... | collective-permute-start | bytes 9224 | tf_op jit(solution)/shard_map/cond/branch_2_fun/ppermute | solution.py:31
  8.4 20.9 %collective-permute-done.13 = f32[1,768]{1,0:T(1,128)} collective-permute-done((f32[1,768]{1,0:T(1,128)}, f32[1,768]{1,0:T(1,128)}, u32[]{:S(2)}, u32[]{:S(2)}) %collective-permute-start.13) | collective-permute-done | bytes 3104 | tf_op jit(solution)/shard_map/cond/branch_2_fun/ppermute | solution.py:31
  29.4 0.0 collective-permute-done.14
  29.4 0.0 collective-permute-done.11
  29.4 0.0 collective-permute-done.12
  29.4 0.0 collective-permute-done.10
  29.4 9.1 %step.1 = (f32[2176,128]{1,0:T(8,128)S(1)}, f32[12,128]{1,0:T(8,128)S(1)}, f32[2176,128]{1,0:T(8,128)}, f32[1,1536]{1,0:T(1,128)}) custom-call(bf16[2,1,784,512]{3,2,1,0:T(8,128)(2,1)} %refs_1_.3, bf16[2,1,784,512]{3,2,1,0:T(8,128)(2,1)} %refs_2_.1, f32[512,128]{1,0:T(8,128)} %bitcast.20, f32[1152,128]{1,0:T(8,128)} %bitcast.14, f32[512,128]{1,0:T(8,128)} %bitcast.26, ...), custom_call_target="tpu_custom_call" | custom-call | flops 1310195712 | bytes 5451776 | tf_op jit(solution)/shard_map/step/pallas_call | solution.py:458
  38.6 26.1 %conditional.3 = (f32[2176,128]{1,0:T(8,128)}, f32[12,128]{1,0:T(8,128)}) conditional(s32[]{:T(128)} %clamp.7, (f32[2176,128]{1,0:T(8,128)S(1)}, f32[12,128]{1,0:T(8,128)S(1)}) %tuple.52, (f32[2176,128]{1,0:T(8,128)S(1)}, f32[12,128]{1,0:T(8,128)S(1)}) %tuple.52, (f32[2176,128]{1,0:T(8,128)S(1)}, ...), branch_computations={%region_5.6_spmd, %region_6.7_spmd, %region_7.8_spmd, %region_8.9_... | conditional | bytes 4481120 | solution.py:566
  38.6 1.9 %collective-permute-start.31 = (f32[2176,128]{1,0:T(8,128)S(1)}, f32[2176,128]{1,0:T(8,128)}, u32[]{:S(2)}, u32[]{:S(2)}) collective-permute-start(f32[2176,128]{1,0:T(8,128)S(1)} %get-tuple-element.101), channel_id=1, source_target_pairs={{0,8},{1,9},{2,10},{3,11},{4,12},{5,13},{6,14},{7,15},{8,0},{9,1},... | collective-permute-start | bytes 3342344 | tf_op jit(solution)/shard_map/cond/branch_3_fun/ppermute | solution.py:31
  40.4 0.2 collective-permute-start.32
  40.7 24.0 %collective-permute-done.32 = f32[12,128]{1,0:T(8,128)} collective-permute-done((f32[12,128]{1,0:T(8,128)S(1)}, f32[12,128]{1,0:T(8,128)}, u32[]{:S(2)}, u32[]{:S(2)}) %collective-permute-start.32) | collective-permute-done | bytes 6176 | tf_op jit(solution)/shard_map/cond/branch_3_fun/ppermute | solution.py:31
  64.7 0.0 collective-permute-done.31
  64.7 9.7 %last_step.1 = (f32[16,72,128]{2,1,0:T(8,128)}, f32[16,72,128]{2,1,0:T(8,128)}, f32[2176,128]{1,0:T(8,128)}, f32[1,1536]{1,0:T(1,128)}) custom-call(s32[1]{0:T(128)} %bitcast.3.refs_0_, bf16[2,1,784,512]{3,2,1,0:T(8,128)(2,1)} %refs_1_.3, bf16[2,1,784,512]{3,2,1,0:T(8,128)(2,1)} %refs_2_.1, f32[2176,128]{1,0:T(8,128)S(1)} %get-tuple-element.159.refs_3_, ...), custom_call_target="tpu_custom_call" | custom-call | flops 1310195712 | bytes 6572036 | tf_op jit(solution)/shard_map/last_step/pallas_call | solution.py:458
  74.3 0.1 collective-permute-start.35
  74.4 0.0 copy-start.1
  74.4 1.1 %copy-done.1 = f32[16,72,128]{2,1,0:T(8,128)S(1)} copy-done((f32[16,72,128]{2,1,0:T(8,128)S(1)}, f32[16,72,128]{2,1,0:T(8,128)}, u32[]{:S(2)}) %copy-start.1) | copy-done | bytes 589848
  75.5 0.0 copy-start
  75.5 0.1 copy.53.refs_1_
  75.6 1.0 %collective-permute-done.35.refs_2_ = f32[16,72,128]{2,1,0:T(8,128)S(1)} collective-permute-done((f32[16,72,128]{2,1,0:T(8,128)}, f32[16,72,128]{2,1,0:T(8,128)S(1)}, u32[]{:S(2)}, u32[]{:S(2)}) %collective-permute-start.35) | collective-permute-done | bytes 589856 | tf_op jit(solution)/shard_map/ppermute | solution.py:485
  76.6 0.1 fold.3
  76.7 0.0 copy-start.2
  76.7 1.5 %collective-permute-start.36 = (f32[4,72,128]{2,1,0:T(8,128)S(1)}, f32[4,72,128]{2,1,0:T(8,128)S(1)}, u32[]{:S(2)}, u32[]{:S(2)}) collective-permute-start(f32[4,72,128]{2,1,0:T(8,128)S(1)} %get-tuple-element.170), channel_id=1, source_target_pairs={{0,2},{1,3},{2,0},{3,1},{4,6},{5,7},{6,4},{7,5},{8,10},{9,11},{10,... | collective-permute-start | bytes 442376 | tf_op jit(solution)/shard_map/ppermute | solution.py:485
  78.2 1.5 %collective-permute-start.37 = (f32[4,72,128]{2,1,0:T(8,128)S(1)}, f32[4,72,128]{2,1,0:T(8,128)S(1)}, u32[]{:S(2)}, u32[]{:S(2)}) collective-permute-start(f32[4,72,128]{2,1,0:T(8,128)S(1)} %get-tuple-element.171), channel_id=1, source_target_pairs={{0,4},{1,5},{2,6},{3,7},{4,0},{5,1},{6,2},{7,3},{8,12},{9,13},{10,... | collective-permute-start | bytes 442376 | tf_op jit(solution)/shard_map/ppermute | solution.py:485
  79.7 0.6 collective-permute-start.38
  80.3 0.0 copy-done
  80.3 5.1 %pack.2 = (bf16[1,65536]{1,0:T(2,128)(2,1)}, bf16[1,147456]{1,0:T(2,128)(2,1)}) custom-call(f32[2176,128]{1,0:T(8,128)S(1)} %copy-done), custom_call_target="tpu_custom_call" | custom-call | bytes 1114112 | tf_op jit(solution)/shard_map/pack/pallas_call | solution.py:458
  85.4 0.0 collective-permute-done.36.refs_2_
  85.4 1.5 %collective-permute-done.37.refs_3_ = f32[4,72,128]{2,1,0:T(8,128)S(1)} collective-permute-done((f32[4,72,128]{2,1,0:T(8,128)S(1)}, f32[4,72,128]{2,1,0:T(8,128)S(1)}, u32[]{:S(2)}, u32[]{:S(2)}) %collective-permute-start.37) | collective-permute-done | bytes 147488 | tf_op jit(solution)/shard_map/ppermute | solution.py:485
  87.0 0.0 collective-permute-done.38.refs_4_
  87.0 1.6 %collective-permute-start.39 = (f32[2,72,128]{2,1,0:T(8,128)S(1)}, f32[2,72,128]{2,1,0:T(8,128)S(1)}, u32[]{:S(2)}, u32[]{:S(2)}) collective-permute-start(f32[2,72,128]{2,1,0:T(8,128)S(1)} %get-tuple-element.180), channel_id=1, source_target_pairs={{0,8},{1,9},{2,10},{3,11},{4,12},{5,13},{6,14},{7,15},{8,0},{9,1},... | collective-permute-start | bytes 221192 | tf_op jit(solution)/shard_map/ppermute | solution.py:485
  88.7 0.0 copy-done.2
  88.7 2.1 %pack.3 = (bf16[1,65536]{1,0:T(2,128)(2,1)}, bf16[1,1536]{1,0:T(2,128)(2,1)}) custom-call(f32[2176,128]{1,0:T(8,128)S(1)} %copy-done, f32[1,1536]{1,0:T(1,128)S(1)} %copy-done.2), custom_call_target="tpu_custom_call" | custom-call | bytes 1120256 | tf_op jit(solution)/shard_map/pack/pallas_call | solution.py:458
  90.7 0.7 collective-permute-done.39.refs_2_
  91.5 2.7 %collective-permute-start.40 = (f32[1,72,128]{2,1,0:T(8,128)S(1)}, f32[1,72,128]{2,1,0:T(8,128)S(1)}, u32[]{:S(2)}, u32[]{:S(2)}) collective-permute-start(f32[1,72,128]{2,1,0:T(8,128)S(1)} %get-tuple-element.186), channel_id=1, source_target_pairs={{0,16},{1,17},{2,18},{3,19},{4,20},{5,21},{6,22},{7,23},{8,24},{9,... | collective-permute-start | bytes 110600 | tf_op jit(solution)/shard_map/ppermute | solution.py:485
  94.1 2.3 %collective-permute-done.40.refs_1_ = f32[1,72,128]{2,1,0:T(8,128)S(1)} collective-permute-done((f32[1,72,128]{2,1,0:T(8,128)S(1)}, f32[1,72,128]{2,1,0:T(8,128)S(1)}, u32[]{:S(2)}, u32[]{:S(2)}) %collective-permute-start.40) | collective-permute-done | bytes 36896 | tf_op jit(solution)/shard_map/ppermute | solution.py:485
  96.4 0.6 mean.1
  (2 shorter events, 0.1 us)
Async XLA Ops:
  1.3 28.1 %collective-permute-start.10 = (f32[1152,128]{1,0:T(8,128)}, f32[1152,128]{1,0:T(8,128)}, u32[]{:S(2)}, u32[]{:S(2)}) collective-permute-start(f32[1152,128]{1,0:T(8,128)} %get-tuple-element.80), channel_id=1, source_target_pairs={{0,4},{1,5},{2,6},{3,7},{4,0},{5,1},{6,2},{7,3},{8,12},{9,13},{10,... | collective-permute-start | bytes 1769480 | tf_op jit(solution)/shard_map/cond/branch_2_fun/ppermute | solution.py:31
  4.4 25.0 %collective-permute-start.11 = (f32[512,128]{1,0:T(8,128)}, f32[512,128]{1,0:T(8,128)}, u32[]{:S(2)}, u32[]{:S(2)}) collective-permute-start(f32[512,128]{1,0:T(8,128)} %get-tuple-element.81), channel_id=1, source_target_pairs={{0,4},{1,5},{2,6},{3,7},{4,0},{5,1},{6,2},{7,3},{8,12},{9,13},{10,... | collective-permute-start | bytes 786440 | tf_op jit(solution)/shard_map/cond/branch_2_fun/ppermute | solution.py:31
  4.5 24.9 %collective-permute-start.12 = (f32[512,128]{1,0:T(8,128)}, f32[512,128]{1,0:T(8,128)}, u32[]{:S(2)}, u32[]{:S(2)}) collective-permute-start(f32[512,128]{1,0:T(8,128)} %get-tuple-element.82), channel_id=1, source_target_pairs={{0,4},{1,5},{2,6},{3,7},{4,0},{5,1},{6,2},{7,3},{8,12},{9,13},{10,... | collective-permute-start | bytes 786440 | tf_op jit(solution)/shard_map/cond/branch_2_fun/ppermute | solution.py:31
  6.4 23.0 %collective-permute-start.13 = (f32[1,768]{1,0:T(1,128)}, f32[1,768]{1,0:T(1,128)}, u32[]{:S(2)}, u32[]{:S(2)}) collective-permute-start(f32[1,768]{1,0:T(1,128)} %get-tuple-element.83), channel_id=1, source_target_pairs={{0,4},{1,5},{2,6},{3,7},{4,0},{5,1},{6,2},{7,3},{8,12},{9,13},{10,... | collective-permute-start | bytes 9224 | tf_op jit(solution)/shard_map/cond/branch_2_fun/ppermute | solution.py:31
  6.5 22.9 %collective-permute-start.14 = (f32[1,768]{1,0:T(1,128)}, f32[1,768]{1,0:T(1,128)}, u32[]{:S(2)}, u32[]{:S(2)}) collective-permute-start(f32[1,768]{1,0:T(1,128)} %get-tuple-element.84), channel_id=1, source_target_pairs={{0,4},{1,5},{2,6},{3,7},{4,0},{5,1},{6,2},{7,3},{8,12},{9,13},{10,... | collective-permute-start | bytes 9224 | tf_op jit(solution)/shard_map/cond/branch_2_fun/ppermute | solution.py:31
  38.6 26.1 %collective-permute-start.31 = (f32[2176,128]{1,0:T(8,128)S(1)}, f32[2176,128]{1,0:T(8,128)}, u32[]{:S(2)}, u32[]{:S(2)}) collective-permute-start(f32[2176,128]{1,0:T(8,128)S(1)} %get-tuple-element.101), channel_id=1, source_target_pairs={{0,8},{1,9},{2,10},{3,11},{4,12},{5,13},{6,14},{7,15},{8,0},{9,1},... | collective-permute-start | bytes 3342344 | tf_op jit(solution)/shard_map/cond/branch_3_fun/ppermute | solution.py:31
  40.4 24.2 %collective-permute-start.32 = (f32[12,128]{1,0:T(8,128)S(1)}, f32[12,128]{1,0:T(8,128)}, u32[]{:S(2)}, u32[]{:S(2)}) collective-permute-start(f32[12,128]{1,0:T(8,128)S(1)} %get-tuple-element.102), channel_id=1, source_target_pairs={{0,8},{1,9},{2,10},{3,11},{4,12},{5,13},{6,14},{7,15},{8,0},{9,1},... | collective-permute-start | bytes 18440 | tf_op jit(solution)/shard_map/cond/branch_3_fun/ppermute | solution.py:31
  74.3 2.3 %collective-permute-start.35 = (f32[16,72,128]{2,1,0:T(8,128)}, f32[16,72,128]{2,1,0:T(8,128)S(1)}, u32[]{:S(2)}, u32[]{:S(2)}) collective-permute-start(f32[16,72,128]{2,1,0:T(8,128)} %get-tuple-element.165), channel_id=1, source_target_pairs={{0,1},{1,0},{2,3},{3,2},{4,5},{5,4},{6,7},{7,6},{8,9},{9,8},{10,11... | collective-permute-start | bytes 1769480 | tf_op jit(solution)/shard_map/ppermute | solution.py:485
  74.4 1.1 %copy-start.1 = (f32[16,72,128]{2,1,0:T(8,128)S(1)}, f32[16,72,128]{2,1,0:T(8,128)}, u32[]{:S(2)}) copy-start(f32[16,72,128]{2,1,0:T(8,128)} %get-tuple-element.166.source) | copy-start | bytes 1769476
  75.5 4.8 %copy-start = (f32[2176,128]{1,0:T(8,128)S(1)}, f32[2176,128]{1,0:T(8,128)}, u32[]{:S(2)}) copy-start(f32[2176,128]{1,0:T(8,128)} %get-tuple-element.173.refs_0_) | copy-start | bytes 3342340
  76.7 11.9 %copy-start.2 = (f32[1,1536]{1,0:T(1,128)S(1)}, f32[1,1536]{1,0:T(1,128)}, u32[]{:S(2)}) copy-start(f32[1,1536]{1,0:T(1,128)} %get-tuple-element.181.refs_1_) | copy-start | bytes 18436
  76.7 8.7 %collective-permute-start.36 = (f32[4,72,128]{2,1,0:T(8,128)S(1)}, f32[4,72,128]{2,1,0:T(8,128)S(1)}, u32[]{:S(2)}, u32[]{:S(2)}) collective-permute-start(f32[4,72,128]{2,1,0:T(8,128)S(1)} %get-tuple-element.170), channel_id=1, source_target_pairs={{0,2},{1,3},{2,0},{3,1},{4,6},{5,7},{6,4},{7,5},{8,10},{9,11},{10,... | collective-permute-start | bytes 442376 | tf_op jit(solution)/shard_map/ppermute | solution.py:485
  78.2 8.8 %collective-permute-start.37 = (f32[4,72,128]{2,1,0:T(8,128)S(1)}, f32[4,72,128]{2,1,0:T(8,128)S(1)}, u32[]{:S(2)}, u32[]{:S(2)}) collective-permute-start(f32[4,72,128]{2,1,0:T(8,128)S(1)} %get-tuple-element.171), channel_id=1, source_target_pairs={{0,4},{1,5},{2,6},{3,7},{4,0},{5,1},{6,2},{7,3},{8,12},{9,13},{10,... | collective-permute-start | bytes 442376 | tf_op jit(solution)/shard_map/ppermute | solution.py:485
  79.7 7.3 %collective-permute-start.38 = (f32[4,72,128]{2,1,0:T(8,128)S(1)}, f32[4,72,128]{2,1,0:T(8,128)S(1)}, u32[]{:S(2)}, u32[]{:S(2)}) collective-permute-start(f32[4,72,128]{2,1,0:T(8,128)S(1)} %get-tuple-element.172), channel_id=1, source_target_pairs={{0,6},{1,7},{2,4},{3,5},{4,2},{5,3},{6,0},{7,1},{8,14},{9,15},{10,... | collective-permute-start | bytes 442376 | tf_op jit(solution)/shard_map/ppermute | solution.py:485
  87.0 4.4 %collective-permute-start.39 = (f32[2,72,128]{2,1,0:T(8,128)S(1)}, f32[2,72,128]{2,1,0:T(8,128)S(1)}, u32[]{:S(2)}, u32[]{:S(2)}) collective-permute-start(f32[2,72,128]{2,1,0:T(8,128)S(1)} %get-tuple-element.180), channel_id=1, source_target_pairs={{0,8},{1,9},{2,10},{3,11},{4,12},{5,13},{6,14},{7,15},{8,0},{9,1},... | collective-permute-start | bytes 221192 | tf_op jit(solution)/shard_map/ppermute | solution.py:485
  91.5 4.9 %collective-permute-start.40 = (f32[1,72,128]{2,1,0:T(8,128)S(1)}, f32[1,72,128]{2,1,0:T(8,128)S(1)}, u32[]{:S(2)}, u32[]{:S(2)}) collective-permute-start(f32[1,72,128]{2,1,0:T(8,128)S(1)} %get-tuple-element.186), channel_id=1, source_target_pairs={{0,16},{1,17},{2,18},{3,19},{4,20},{5,21},{6,22},{7,23},{8,24},{9,... | collective-permute-start | bytes 110600 | tf_op jit(solution)/shard_map/ppermute | solution.py:485
